TPU v7x, 512 devices: a whole 4x8x8 slice. The times are simulated.
512 devices in a mesh: resp: 16 (over y_hi, z), heads: 8 (over x, core), prompt: 4 (over y_lo).
Axes of the slice: x: 4, y: 8 (y_hi: 2, y_lo: 4; y = y_hi * 4 + y_lo), z: 8, core: 2. Of those that a mesh axis runs over, the one named last changes fastest.
Arguments:
- queries: bfloat16 [64, 512, 8192], P(('resp', 'prompt'), 'heads'), may hold values from -8 to 8
- outputs: bfloat16 [64, 512, 8192], P(('resp', 'prompt'), 'heads'), may hold values from -6 to 6
- out_grads: bfloat16 [64, 512, 8192], P(('resp', 'prompt'), 'heads'), may hold values from -24 to 24
- resp_keys: bfloat16 [64, 512, 1024], P(('resp', 'prompt'), 'heads'), may hold values from -6 to 6
- resp_values: bfloat16 [64, 512, 1024], P(('resp', 'prompt'), 'heads'), may hold values from -6 to 6
- prompt_keys: bfloat16 [512, 4, 1024], P(('resp', 'prompt'), None, 'heads'), may hold values from -8 to 8
- prompt_values: bfloat16 [512, 4, 1024], P(('resp', 'prompt'), None, 'heads'), may hold values from -6 to 6
- prompt_of: int32 [64], P(('resp', 'prompt')), may hold values from 0 to 3
- lengths: int32 [64], P(('resp', 'prompt')), may hold values from 64 to 512, as said below
Outputs:
- query_grads: bfloat16 [64, 512, 8192], P(('resp', 'prompt'), 'heads')
- resp_key_grads: bfloat16 [64, 512, 1024], P(('resp', 'prompt'), 'heads')
- resp_value_grads: bfloat16 [64, 512, 1024], P(('resp', 'prompt'), 'heads')
- prompt_key_grads: bfloat16 [512, 4, 1024], P(('resp', 'prompt'), None, 'heads')
- prompt_value_grads: bfloat16 [512, 4, 1024], P(('resp', 'prompt'), None, 'heads')
Inputs may be any that keep to these rules, and one draw needn't show every extreme that they name: `lengths`: some response has exactly 512 live tokens.
All inputs are finite; a program needn't handle non-finite values.
Results may differ from a plain program's by a relative error of at most 0.0055.
Values may be sent and summed in bfloat16 or wider, within the bound.
A program may use at most 64 MiB of HBM per device.

v0:
```python
import jax
import jax.numpy as jnp
from jax import lax
from jax.sharding import PartitionSpec as P

HD = 128


PAIR = 2


def block_grads(query_blk, output_blk, grad_live, prompt_k, prompt_v, own_k, own_v):
    wide = jnp.float32
    scale = HD ** (-0.5)
    rows = query_blk.shape[0]
    score_p = scale * jnp.einsum("rhd,pd->hrp", query_blk, prompt_k, preferred_element_type=wide)
    score_r = scale * jnp.einsum("rhd,jd->hrj", query_blk, own_k, preferred_element_type=wide)
    causal = lax.broadcasted_iota(jnp.int32, (rows, rows), 0) >= lax.broadcasted_iota(
        jnp.int32, (rows, rows), 1
    )
    score_r = jnp.where(causal[None], score_r, -jnp.inf)
    peak = jnp.maximum(jnp.max(score_p, -1), jnp.max(score_r, -1))
    total = jnp.sum(jnp.exp(score_p - peak[..., None]), -1) + jnp.sum(
        jnp.exp(score_r - peak[..., None]), -1
    )
    log_total = peak + jnp.log(total)
    prob_p = jnp.exp(score_p - log_total[..., None])
    prob_r = jnp.exp(score_r - log_total[..., None])
    delta = jnp.einsum("rhd,rhd->hr", grad_live, output_blk, preferred_element_type=wide)
    dprob_p = jnp.einsum("rhd,pd->hrp", grad_live, prompt_v, preferred_element_type=wide)
    dprob_r = jnp.einsum("rhd,jd->hrj", grad_live, own_v, preferred_element_type=wide)
    dscore_p = (prob_p * (dprob_p - delta[..., None])).astype(jnp.bfloat16)
    dscore_r = (prob_r * (dprob_r - delta[..., None])).astype(jnp.bfloat16)
    prob_pb = prob_p.astype(jnp.bfloat16)
    prob_rb = prob_r.astype(jnp.bfloat16)
    dquery = scale * (
        jnp.einsum("hrp,pd->rhd", dscore_p, prompt_k, preferred_element_type=wide)
        + jnp.einsum("hrj,jd->rhd", dscore_r, own_k, preferred_element_type=wide)
    )
    dkey_p = scale * jnp.einsum("hrp,rhd->pd", dscore_p, query_blk, preferred_element_type=wide)
    dval_p = jnp.einsum("hrp,rhd->pd", prob_pb, grad_live, preferred_element_type=wide)
    dkey_r = scale * jnp.einsum("hrj,rhd->jd", dscore_r, query_blk, preferred_element_type=wide)
    dval_r = jnp.einsum("hrj,rhd->jd", prob_rb, grad_live, preferred_element_type=wide)
    return (dquery, dkey_p, dval_p, dkey_r, dval_r)


def add_into(target, update):
    return target + update


def respond(
    query_all, output_all, grad_all, key_own, value_own, prompt_ids, key_prompt, value_prompt
):
    resp_count = query_all.shape[0]
    rows = query_all.shape[1]
    kv_local = key_own.shape[2] // HD
    group = query_all.shape[2] // (kv_local * HD)
    pairs = group // PAIR
    prompt_len = key_prompt.shape[0]
    steps = resp_count * kv_local * pairs

    def visit(carry, index):
        dq_all, own_dk, own_dv, term_k, term_v = carry
        resp_idx = index // (kv_local * pairs)
        kv_head = index // pairs % kv_local
        head_pair = index % pairs
        column = (kv_head * group + head_pair * PAIR) * HD
        kv_col = kv_head * HD

        def pick(source):
            return lax.dynamic_slice(source, (resp_idx, 0, column), (1, rows, PAIR * HD)).reshape(
                rows, PAIR, HD
            )

        def pick_own(source):
            return source.reshape(rows, HD)

        prompt_id = prompt_ids[resp_idx]

        def pick_prompt(source):
            return lax.dynamic_slice(source, (0, prompt_id, kv_col), (prompt_len, 1, HD)).reshape(
                prompt_len, HD
            )

        dquery, dkey_p, dval_p, dkey_r, dval_r = block_grads(
            pick(query_all),
            pick(output_all),
            pick(grad_all),
            pick_prompt(key_prompt),
            pick_prompt(value_prompt),
            pick_own(key_own),
            pick_own(value_own),
        )
        dq_all = lax.dynamic_update_slice(
            dq_all, dquery.astype(jnp.bfloat16).reshape(1, rows, PAIR * HD), (resp_idx, 0, column)
        )
        own_dk = add_into(own_dk, dkey_r.reshape(1, rows, HD))
        own_dv = add_into(own_dv, dval_r.reshape(1, rows, HD))
        term_k = add_into(term_k, dkey_p.reshape(1, prompt_len, HD))
        term_v = add_into(term_v, dval_p.reshape(1, prompt_len, HD))
        return ((dq_all, own_dk, own_dv, term_k, term_v), None)

    term_shape = (resp_count, prompt_len, kv_local * HD)
    start = (
        jnp.zeros(query_all.shape, jnp.bfloat16),
        jnp.zeros(key_own.shape, jnp.float32),
        jnp.zeros(key_own.shape, jnp.float32),
        jnp.zeros(term_shape, jnp.float32),
        jnp.zeros(term_shape, jnp.float32),
    )
    finished, unused = lax.scan(visit, start, jnp.arange(steps, dtype=jnp.int32))
    dq_all, own_dk, own_dv, term_k, term_v = finished
    return (dq_all, own_dk.astype(jnp.bfloat16), own_dv.astype(jnp.bfloat16), term_k, term_v)


def spread_terms(prompt_ids, terms, prompt_count):
    onehot = (prompt_ids[:, None] == jnp.arange(prompt_count, dtype=jnp.int32)[None, :]).astype(
        jnp.float32
    )
    return jnp.einsum("mc,mpd->pcd", onehot, terms, precision=lax.Precision.HIGHEST)


def on_device(
    queries,
    outputs,
    out_grads,
    resp_keys,
    resp_values,
    prompt_keys,
    prompt_values,
    prompt_of,
    lengths,
):
    rows_local = queries.shape[1]
    positions = lax.axis_index("heads") * rows_local + jnp.arange(rows_local, dtype=jnp.int32)
    live = positions[None, :] < lengths[:, None]
    grad_masked = jnp.where(live[:, :, None], out_grads, jnp.zeros_like(out_grads))
    key_prompt, value_prompt = (
        lax.all_gather(prompt_keys, ("resp", "prompt"), axis=0, tiled=True),
        lax.all_gather(prompt_values, ("resp", "prompt"), axis=0, tiled=True),
    )
    prompt_count = key_prompt.shape[1]
    query_all, output_all, grad_all, key_own, value_own = (
        lax.all_to_all(queries, "heads", split_axis=2, concat_axis=1, tiled=True),
        lax.all_to_all(outputs, "heads", split_axis=2, concat_axis=1, tiled=True),
        lax.all_to_all(grad_masked, "heads", split_axis=2, concat_axis=1, tiled=True),
        lax.all_to_all(resp_keys, "heads", split_axis=2, concat_axis=1, tiled=True),
        lax.all_to_all(resp_values, "heads", split_axis=2, concat_axis=1, tiled=True),
    )
    dq_all, own_dk, own_dv, term_k, term_v = respond(
        query_all, output_all, grad_all, key_own, value_own, prompt_of, key_prompt, value_prompt
    )
    query_back, key_back, value_back = (
        lax.all_to_all(dq_all, "heads", split_axis=1, concat_axis=2, tiled=True),
        lax.all_to_all(own_dk, "heads", split_axis=1, concat_axis=2, tiled=True),
        lax.all_to_all(own_dv, "heads", split_axis=1, concat_axis=2, tiled=True),
    )
    dense_k = spread_terms(prompt_of, term_k, prompt_count)
    dense_v = spread_terms(prompt_of, term_v, prompt_count)
    sum_k, sum_v = (
        lax.psum_scatter(dense_k, ("resp", "prompt"), scatter_dimension=0, tiled=True),
        lax.psum_scatter(dense_v, ("resp", "prompt"), scatter_dimension=0, tiled=True),
    )
    return (
        query_back,
        key_back,
        value_back,
        sum_k.astype(jnp.bfloat16),
        sum_v.astype(jnp.bfloat16),
    )


def solution(mesh):
    return jax.shard_map(
        on_device,
        mesh=mesh,
        in_specs=(
            P(("resp", "prompt"), "heads", None),
            P(("resp", "prompt"), "heads", None),
            P(("resp", "prompt"), "heads", None),
            P(("resp", "prompt"), "heads", None),
            P(("resp", "prompt"), "heads", None),
            P(("resp", "prompt"), None, "heads"),
            P(("resp", "prompt"), None, "heads"),
            P(("resp", "prompt")),
            P(("resp", "prompt")),
        ),
        out_specs=(
            P(("resp", "prompt"), "heads", None),
            P(("resp", "prompt"), "heads", None),
            P(("resp", "prompt"), "heads", None),
            P(("resp", "prompt"), None, "heads"),
            P(("resp", "prompt"), None, "heads"),
        ),
        check_vma=False,
    )
```

profile of v0, /device:TPU:262, one launch (start us, length us, event | category | flops | bytes accessed | tf_op | source)
XLA Modules:
  0.0 1001.1 jit_solution(4554937789733141191)
XLA Ops:
  0.7 1.3 copy.199
  2.5 2.3 reduce.3
  5.6 4.8 all-to-all-start.1
  10.8 2.3 reduce.6
  14.5 5.4 all-to-all-start.4
  19.9 6.8 copy.196
  26.6 45.2 %reduce.2 = bf16[8192,64]{1,0:T(8,128)(2,1)S(1)} reduce(bf16[8192,1,64]{2,1,0:T(2,128)(2,1)} %bitcast.318, bf16[]{:T(256)} %broadcast.120), dimensions={1}, to_apply=%bitcast.179.reduce_sub_computation | reduce | bytes 2097154
  71.9 2.7 reshape.227
  74.6 4.8 all-to-all-start
  80.7 152.4 %all_gather.6 = bf16[512,4,128]{2,1,0:T(4,128)(2,1)S(1)} all-gather(bf16[8,4,128]{2,1,0:T(4,128)(2,1)S(1)} %copy-done.4), channel_id=1, replica_groups=mesh['resp'=16,'heads'=8,'prompt'=4] {'resp','prompt'}, dimensions={0}, use_global_device_ids=true | all-gather | bytes 532480 | tf_op jit(solution)/shard_map/all_gather | solution.py:139
  233.5 9.2 copy.206
  242.6 46.5 %reduce.5 = bf16[8192,64]{1,0:T(8,128)(2,1)} reduce(bf16[8192,1,64]{2,1,0:T(2,128)(2,1)} %bitcast.319, bf16[]{:T(256)} %broadcast.120), dimensions={1}, to_apply=%bitcast.185.reduce_sub_computation | reduce | bytes 2097154
  289.2 4.3 reshape.233
  293.5 9.2 copy.202
  302.7 5.0 all-to-all-start.3
  307.7 8.4 fusion.37
  316.1 46.5 %reduce.4 = bf16[8192,64]{1,0:T(8,128)(2,1)} reduce(bf16[8192,1,64]{2,1,0:T(2,128)(2,1)} %fusion.37, bf16[]{:T(256)} %broadcast.120), dimensions={1}, to_apply=%fusion.37.reduce_sub_computation | reduce | bytes 2097154
  362.7 4.3 reshape.231
  367.0 149.5 %all_gather.7 = bf16[512,4,128]{2,0,1:T(8,128)(2,1)S(1)} all-gather(bf16[8,4,128]{2,0,1:T(8,128)(2,1)S(1)} %copy.205), channel_id=1, replica_groups=mesh['resp'=16,'heads'=8,'prompt'=4] {'resp','prompt'}, dimensions={0}, use_global_device_ids=true | all-gather | bytes 532480 | tf_op jit(solution)/shard_map/all_gather | solution.py:140
  517.2 5.3 all-to-all-start.2
  523.4 4.3 reshape.228
  527.7 8.2 copy.197
  537.2 6.5 reshape.234
  543.7 8.9 copy.207
  552.6 1.8 copy.256
  554.5 1.6 copy.208
  556.1 6.5 reshape.232
  562.6 8.9 copy.203
  571.4 1.8 copy.255
  573.3 1.6 copy.204
  576.0 45.2 %while.23 = (s32[]{:T(128)}, bf16[1,512,1024]{1,2,0:T(8,128)(2,1)}, f32[1,512,128]{2,1,0:T(8,128)S(1)}, f32[1,512,128]{2,1,0:T(8,128)S(1)}, f32[1,512,128]{2,1,0...) while((s32[]{:T(128)}, bf16[1,512,1024]{1,2,0:T(8,128)(2,1)}, ...), condition=%wide.region_5.6_spmd.clone, body=%wide.region_0.5_spmd.clone.sunk | while | flops 1356462080 | bytes 43602352 | solution.py:111
  578.9 1.1 constant_dynamic-slice_fusion.8
  590.1 1.1 constant_dynamic-slice_fusion.8
  601.4 1.1 constant_dynamic-slice_fusion.8
  612.7 1.1 constant_dynamic-slice_fusion.8
  621.4 1.4 reduce.9
  623.5 4.8 all-to-all-start.6
  628.5 1.4 reduce.8
  630.6 1.7 all-to-all-done.6
  632.4 5.4 all-to-all-start.7
  637.7 1.3 dynamic-slice
  639.7 4.7 copy.216
  644.4 7.8 reduce.7
  652.2 2.6 reshape.237
  654.8 4.8 all-to-all-start.5
  660.0 332.8 %all-reduce.4 = (bf16[512,4,128]{2,1,0:T(4,128)(2,1)S(1)}, bf16[512,4,128]{2,1,0:T(4,128)(2,1)}) all-reduce(f32[512,4,128]{2,1,0:T(4,128)S(1)} %get-tuple-element.476, f32[512,4,128]{2,1,0:T(4,128)S(1)} %get-tuple-element.475), channel_id=2, replica_groups=mesh['resp'=16,'heads'=8,'prompt'=4] {'resp','prompt'}, use_global_device_ids=true, to_apply=%region_6.7.clone | all-reduce | flops 524288 | bytes 3145728
  992.8 1.3 dynamic-slice_convert_fusion
  995.2 4.3 reshape.238
  (169 shorter events, 44.6 us)
Async XLA Ops:
  0.6 9.8 copy-start.3
  0.6 19.2 %copy-start.2 = (bf16[1,64,8192]{2,1,0:T(8,128)(2,1)S(1)}, bf16[1,64,8192]{2,1,0:T(8,128)(2,1)}, u32[]{:S(2)}) copy-start(bf16[1,64,8192]{2,1,0:T(8,128)(2,1)} %param.11) | copy-start | bytes 3145732
  5.6 8.8 all-to-all-start.1
  14.5 60.1 %all-to-all-start.4 = ((bf16[8,2,4096]{2,1,0:T(2,128)(2,1)}), bf16[8,2,4096]{2,1,0:T(2,128)(2,1)S(1)}, u32[]{:S(2)}, u32[]{:S(2)}) async-start(bf16[8,2,4096]{2,1,0:T(2,128)(2,1)} %reshape.235), calls=%async_computation.4 | async-start | bytes 262144 | tf_op jit(solution)/shard_map/all_to_all | solution.py:148
  71.9 8.8 copy-start.5
  71.9 8.8 copy-start.4
  74.6 228.1 %all-to-all-start = ((bf16[8,2,32768]{2,1,0:T(2,128)(2,1)}), bf16[8,2,32768]{2,1,0:T(2,128)(2,1)S(1)}, u32[]{:S(2)}, u32[]{:S(2)}) async-start(bf16[8,2,32768]{2,1,0:T(2,128)(2,1)} %reshape.227), calls=%async_computation | async-start | bytes 2097152 | tf_op jit(solution)/shard_map/all_to_all | solution.py:144
  302.7 214.5 %all-to-all-start.3 = ((bf16[8,2,32768]{2,1,0:T(2,128)(2,1)}), bf16[8,2,32768]{2,1,0:T(2,128)(2,1)}, u32[]{:S(2)}, u32[]{:S(2)}) async-start(bf16[8,2,32768]{2,1,0:T(2,128)(2,1)} %reshape.233), calls=%async_computation.3 | async-start | bytes 2097152 | tf_op jit(solution)/shard_map/all_to_all | solution.py:145
  517.2 38.9 %all-to-all-start.2 = ((bf16[8,2,32768]{2,1,0:T(2,128)(2,1)}), bf16[8,2,32768]{2,1,0:T(2,128)(2,1)}, u32[]{:S(2)}, u32[]{:S(2)}) async-start(bf16[8,2,32768]{2,1,0:T(2,128)(2,1)} %reshape.231), calls=%async_computation.2 | async-start | bytes 2097152 | tf_op jit(solution)/shard_map/all_to_all | solution.py:146
  576.0 2.8 copy-start
  585.7 1.5 copy-start.1
  587.2 2.8 copy-start
  596.9 1.5 copy-start.1
  598.5 2.8 copy-start
  608.2 1.5 copy-start.1
  609.7 2.8 copy-start
  619.5 1.5 copy-start.1
  623.5 8.9 all-to-all-start.6
  632.4 22.5 %all-to-all-start.7 = ((bf16[8,2,4096]{2,1,0:T(2,128)(2,1)}), bf16[8,2,4096]{2,1,0:T(2,128)(2,1)S(1)}, u32[]{:S(2)}, u32[]{:S(2)}) async-start(bf16[8,2,4096]{2,1,0:T(2,128)(2,1)} %reshape.241), calls=%async_computation.7 | async-start | bytes 262144 | tf_op jit(solution)/shard_map/all_to_all | solution.py:156
  654.8 340.3 %all-to-all-start.5 = ((bf16[8,2,32768]{2,1,0:T(2,128)(2,1)}), bf16[8,2,32768]{2,1,0:T(2,128)(2,1)}, u32[]{:S(2)}, u32[]{:S(2)}) async-start(bf16[8,2,32768]{2,1,0:T(2,128)(2,1)} %reshape.237), calls=%async_computation.5 | async-start | bytes 2097152 | tf_op jit(solution)/shard_map/all_to_all | solution.py:154
where the time goes:
time: 1010 us; the launch traced here: 1000 us
  blocking collectives  635 us (63%)
  other arithmetic  168 us (17%)
  local copies, waits for them, and re-layouts  126 us (12%)
  starting transfers between devices  40.2 us (4%)
  matrix products  18.5 us (2%)
    unnamed x1, blocking collectives  333 us
    unnamed x13, other arithmetic  162 us
    all_gather x1, blocking collectives, on_device(): lax.all_gather(prompt_keys, ('resp', 'prompt'), axis=0, tiled=True)  152 us
    all_gather x1, blocking collectives, on_device(): lax.all_gather(prompt_values, ('resp', 'prompt'), axis=0, tiled=True)  149 us
    unnamed x42, local copies, waits for them, and re-layouts  73.2 us
  transfers between devices with their start and end apart: 8, of which 2 were waited for; matrix products, arithmetic and copies ran while one was open for 24% of the time, Pallas kernels for 0%

commit v1 on v0

v1 whole, which is shorter than its diff:
```python
import functools

import jax
import jax.numpy as jnp
from jax import lax
from jax.experimental import pallas as pl
from jax.experimental.pallas import tpu as pltpu
from jax.sharding import PartitionSpec as P

HD = 128
LOG2E = 1.4426950408889634
WIDE = jnp.float32
HALF = jnp.bfloat16
NT = (((1,), (1,)), ((), ()))
NN = (((1,), (0,)), ((), ()))


def dot(a, b, dims):
    return lax.dot_general(a, b, dims, preferred_element_type=WIDE)


def kernel(
    sizes,
    prompt_id,
    length,
    q_in,
    o_in,
    g_in,
    k_in,
    v_in,
    pkv_in,
    dq_out,
    dk_out,
    dv_out,
    dpkv_out,
    q_all,
    g_all,
    k_all,
    v_all,
    o_mine,
    g_mine,
    delta_send,
    delta_all,
    id_send,
    id_all,
    quarter,
    chosen,
    pkv_all,
    kt,
    pkt,
    dq_all,
    dk_acc,
    dv_acc,
    dpk_acc,
    dpv_acc,
    dk_half,
    dv_half,
    term_send,
    term_all,
    dense,
    dense_all,
    send,
    recv_id,
    recv_quarter,
    recv_pkv,
    recv_kv,
    recv_delta,
    recv_q,
    recv_g,
    recv_dq,
    recv_dkv,
    recv_term,
    recv_dense,
    local,
):
    heads, resps, prompts, group, rows, stages, row_block, own_tokens, prompt_count = sizes
    me = lax.axis_index("heads")
    mine_r = lax.axis_index("resp")
    mine_p = lax.axis_index("prompt")
    total_rows = heads * rows
    width = group * HD
    per_stage = group // stages
    stage_width = per_stage * HD
    span = own_tokens * prompts
    scale = HD**-0.5

    def start(src, dst, send_sem, recv_sem, axis, index):
        pltpu.make_async_remote_copy(
            src_ref=src,
            dst_ref=dst,
            send_sem=send_sem,
            recv_sem=recv_sem,
            device_id={axis: index},
            device_id_type=pl.DeviceIdType.MESH,
        ).start()

    def landed(ref, sem):
        pltpu.make_async_copy(ref, ref, sem).wait()

    def others(count, own, body):
        def step(i, carry):
            body(lax.rem(own + i, count))
            return carry

        lax.fori_loop(1, count, step, 0)

    load_o = pltpu.make_async_copy(o_in, o_mine, local.at[0])
    load_g = pltpu.make_async_copy(g_in, g_mine, local.at[1])
    load_o.start()
    load_g.start()
    own_cols = pl.ds(pl.multiple_of(me * width, width), width)
    own_rows = pl.ds(pl.multiple_of(me * rows, rows), rows)
    own_head = pl.ds(pl.multiple_of(me * HD, HD), HD)
    keep = [
        pltpu.make_async_copy(q_in.at[:, own_cols], q_all.at[own_rows, :], local.at[2]),
        pltpu.make_async_copy(g_in.at[:, own_cols], g_all.at[own_rows, :], local.at[3]),
        pltpu.make_async_copy(k_in.at[:, own_head], k_all.at[own_rows, :], local.at[4]),
        pltpu.make_async_copy(v_in.at[:, own_head], v_all.at[own_rows, :], local.at[5]),
    ]
    for copy in keep:
        copy.start()

    barrier = pltpu.get_barrier_semaphore()
    for axis, count, own in (("heads", heads, me), ("resp", resps, mine_r), ("prompt", prompts, mine_p)):

        def greet(peer, axis=axis):
            pl.semaphore_signal(
                barrier, inc=1, device_id={axis: peer}, device_id_type=pl.DeviceIdType.MESH
            )

        others(count, own, greet)
    id_tile = jnp.full((8, HD), prompt_id[0], jnp.int32).astype(WIDE)
    id_send[...] = id_tile
    id_all[mine_r] = id_tile
    quarter[mine_p] = pkv_in[...]
    pl.semaphore_wait(barrier, heads + resps + prompts - 3)

    others(resps, mine_r, lambda p: start(id_send, id_all.at[mine_r], send.at[0], recv_id, "resp", p))
    others(
        prompts,
        mine_p,
        lambda p: start(pkv_in, quarter.at[mine_p], send.at[1], recv_quarter, "prompt", p),
    )

    def send_kv(p):
        cols = pl.ds(pl.multiple_of(p * HD, HD), HD)
        start(k_in.at[:, cols], k_all.at[own_rows, :], send.at[2], recv_kv.at[0], "heads", p)
        start(v_in.at[:, cols], v_all.at[own_rows, :], send.at[3], recv_kv.at[1], "heads", p)

    others(heads, me, send_kv)

    def send_stage(stage):
        to = pl.ds(pl.multiple_of(stage * stage_width, stage_width), stage_width)

        def body(p):
            cols = pl.ds(pl.multiple_of(p * width + stage * stage_width, stage_width), stage_width)
            start(q_in.at[:, cols], q_all.at[own_rows, to], send.at[4], recv_q.at[stage], "heads", p)
            start(g_in.at[:, cols], g_all.at[own_rows, to], send.at[5], recv_g.at[stage], "heads", p)

        others(heads, me, body)

    send_stage(0)

    landed(quarter.at[pl.ds(0, prompts - 1)], recv_quarter)
    landed(id_all.at[pl.ds(0, resps - 1)], recv_id)
    held = [quarter[b].astype(WIDE) for b in range(prompts)]
    part = prompt_count * own_tokens

    def pick(kv, c):
        lo = kv * part + c * own_tokens
        return jnp.concatenate([h[lo : lo + own_tokens] for h in held], axis=0)

    by_prompt = [jnp.concatenate([pick(0, c), pick(1, c)], axis=0) for c in range(prompt_count)]

    def weights(index):
        return [(id_all[index] == float(c)).astype(WIDE)[0:1] for c in range(prompt_count)]

    def choose(p):
        w = weights(p)
        out = w[0] * by_prompt[0]
        for c in range(1, prompt_count):
            out = out + w[c] * by_prompt[c]
        return out.astype(HALF)

    def send_prompt(p):
        chosen[p] = choose(p)
        start(chosen.at[p], pkv_all.at[mine_r], send.at[6], recv_pkv, "resp", p)

    others(resps, mine_r, send_prompt)
    pkv_all[mine_r] = choose(mine_r)

    load_o.wait()
    load_g.wait()
    head_of = lax.broadcasted_iota(jnp.int32, (group, width), 1) // HD
    ones = (head_of == lax.broadcasted_iota(jnp.int32, (group, width), 0)).astype(HALF)
    side = lax.rem(me, 2)
    first = (lax.broadcasted_iota(jnp.int32, (group, 2 * rows), 1) // rows) == side

    def delta_for(p):
        cols = pl.ds(pl.multiple_of(p * width, width), width)
        prod = o_mine[:, cols].astype(WIDE) * g_mine[:, cols].astype(WIDE)
        high = prod.astype(HALF)
        low = (prod - high.astype(WIDE)).astype(HALF)
        d = dot(ones, high, NT) + dot(ones, low, NT)
        return jnp.where(first, jnp.concatenate([d, d], axis=1), 0.0)

    def send_delta(p):
        delta_send[p] = delta_for(p)
        start(delta_send.at[p], delta_all.at[me], send.at[7], recv_delta, "heads", p)

    others(heads, me, send_delta)
    delta_all[me] = delta_for(me)

    def rest(stage, carry):
        send_stage(stage)
        return carry

    lax.fori_loop(1, stages, rest, 0)

    dk_acc[...] = jnp.zeros_like(dk_acc)
    dv_acc[...] = jnp.zeros_like(dv_acc)
    dpk_acc[...] = jnp.zeros_like(dpk_acc)
    dpv_acc[...] = jnp.zeros_like(dpv_acc)
    for copy in keep:
        copy.wait()
    landed(k_all.at[pl.ds(0, total_rows - rows)], recv_kv.at[0])
    landed(v_all.at[pl.ds(0, total_rows - rows)], recv_kv.at[1])
    landed(delta_all.at[pl.ds(0, heads - 1)], recv_delta)
    landed(pkv_all.at[pl.ds(0, resps - 1)], recv_pkv)
    prompt_len = resps * span
    kt[...] = k_all[...].T
    pkt[...] = pkv_all[:, 0:span, :].reshape(prompt_len, HD).T
    delta_rows = jnp.concatenate(
        [delta_all[2 * i] + delta_all[2 * i + 1] for i in range(heads // 2)], axis=1
    )
    live = (lax.broadcasted_iota(jnp.int32, (1, total_rows), 1) < length[0]).astype(WIDE)
    causal = lax.broadcasted_iota(jnp.int32, (row_block, row_block), 0) <= lax.broadcasted_iota(
        jnp.int32, (row_block, row_block), 1
    )

    def one_block(head_in_group, delta_head, block):
        cols = pl.ds(pl.multiple_of(head_in_group * HD, HD), HD)
        lo = block * row_block
        at = slice(lo, lo + row_block)
        keys = lo + row_block
        q = q_all[lo : lo + row_block, cols]
        g = g_all[lo : lo + row_block, cols]
        pk = pkv_all[:, 0:span, :].reshape(prompt_len, HD)
        pv = pkv_all[:, span : 2 * span, :].reshape(prompt_len, HD)
        score_p = dot(pk, q, NT)
        score_r = dot(k_all[0:keys, :], q, NT)
        diag = jnp.where(causal, score_r[lo:keys], -jnp.inf)
        score_r = diag if lo == 0 else jnp.concatenate([score_r[0:lo], diag], axis=0)
        peak = jnp.maximum(
            jnp.max(score_p, axis=0, keepdims=True), jnp.max(score_r, axis=0, keepdims=True)
        )
        e_p = jnp.exp2((score_p - peak) * (scale * LOG2E))
        e_r = jnp.exp2((score_r - peak) * (scale * LOG2E))
        total = jnp.sum(e_p, axis=0, keepdims=True) + jnp.sum(e_r, axis=0, keepdims=True)
        norm = live[:, at] / total
        prob_p = e_p * norm
        prob_r = e_r * norm
        d = delta_head[:, at]
        ds_p = (prob_p * (dot(pv, g, NT) - d)).astype(HALF)
        ds_r = (prob_r * (dot(v_all[0:keys, :], g, NT) - d)).astype(HALF)
        prob_p = prob_p.astype(HALF)
        prob_r = prob_r.astype(HALF)
        dpv_acc[...] += dot(prob_p, g, NN)
        dv_acc[0:keys, :] += dot(prob_r, g, NN)
        dpk_acc[...] += dot(ds_p, q, NN)
        dk_acc[0:keys, :] += dot(ds_r, q, NN)
        dq_t = dot(pkt[...], ds_p, NN) + dot(kt[:, 0:keys], ds_r, NN)
        dq_all[lo : lo + row_block, cols] = (dq_t * scale).T.astype(HALF)

    def visit(stage, carry):
        landed(q_all.at[pl.ds(0, total_rows - rows), pl.ds(0, stage_width)], recv_q.at[stage])
        landed(g_all.at[pl.ds(0, total_rows - rows), pl.ds(0, stage_width)], recv_g.at[stage])
        for sub in range(per_stage):
            head_in_group = stage * per_stage + sub
            pick_head = (
                lax.broadcasted_iota(jnp.int32, (group, total_rows), 0) == head_in_group
            ).astype(WIDE)
            delta_head = jnp.sum(delta_rows * pick_head, axis=0, keepdims=True)
            for block in range(total_rows // row_block):
                one_block(head_in_group, delta_head, block)
        src_cols = pl.ds(pl.multiple_of(stage * stage_width, stage_width), stage_width)
        dst_cols = pl.ds(pl.multiple_of(me * width + stage * stage_width, stage_width), stage_width)

        def give(p):
            part_rows = pl.ds(pl.multiple_of(p * rows, rows), rows)
            start(
                dq_all.at[part_rows, src_cols],
                dq_out.at[:, dst_cols],
                send.at[8],
                recv_dq,
                "heads",
                p,
            )

        others(heads, me, give)
        return carry

    lax.fori_loop(0, stages, visit, 0)

    for a in range(resps):
        lo = a * span
        term_send[a] = jnp.concatenate(
            [dpk_acc[lo : lo + span, :] * scale, dpv_acc[lo : lo + span, :]], axis=0
        ).astype(HALF)
    others(
        resps,
        mine_r,
        lambda p: start(term_send.at[p], term_all.at[mine_r], send.at[9], recv_term, "resp", p),
    )
    dk_half[...] = (dk_acc[...] * scale).astype(HALF)
    dv_half[...] = dv_acc[...].astype(HALF)

    def give_own(p):
        part_rows = pl.ds(pl.multiple_of(p * rows, rows), rows)
        start(dk_half.at[part_rows, :], dk_out.at[:, own_head], send.at[10], recv_dkv.at[0], "heads", p)
        start(dv_half.at[part_rows, :], dv_out.at[:, own_head], send.at[11], recv_dkv.at[1], "heads", p)

    others(heads, me, give_own)
    put = [
        pltpu.make_async_copy(dq_all.at[own_rows, :], dq_out.at[:, own_cols], local.at[0]),
        pltpu.make_async_copy(dk_half.at[own_rows, :], dk_out.at[:, own_head], local.at[1]),
        pltpu.make_async_copy(dv_half.at[own_rows, :], dv_out.at[:, own_head], local.at[2]),
    ]
    for copy in put:
        copy.start()
    term_all[mine_r] = term_send[mine_r]
    landed(term_all.at[pl.ds(0, resps - 1)], recv_term)
    sums = [jnp.zeros((2 * span, HD), WIDE) for c in range(prompt_count)]
    for a in range(resps):
        w = weights(a)
        term = term_all[a].astype(WIDE)
        sums = [s + w[c] * term for c, s in enumerate(sums)]
    for b in range(prompts):
        pieces = []
        for kv in range(2):
            for c in range(prompt_count):
                lo = kv * span + b * own_tokens
                pieces.append(sums[c][lo : lo + own_tokens])
        dense[b] = jnp.concatenate(pieces, axis=0)
    dense_all[mine_p] = dense[mine_p]
    others(
        prompts,
        mine_p,
        lambda p: start(dense.at[p], dense_all.at[mine_p], send.at[12], recv_dense, "prompt", p),
    )
    landed(dense_all.at[pl.ds(0, prompts - 1)], recv_dense)
    result = dense_all[0]
    for b in range(1, prompts):
        result = result + dense_all[b]
    dpkv_out[...] = result

    for copy in put:
        copy.wait()
    far = pl.ds(0, (heads - 1) * width)
    far_kv = pl.ds(0, (heads - 1) * HD)
    landed(dq_out.at[:, far], recv_dq)
    landed(dk_out.at[:, far_kv], recv_dkv.at[0])
    landed(dv_out.at[:, far_kv], recv_dkv.at[1])
    landed(id_all.at[pl.ds(0, resps - 1)], send.at[0])
    landed(quarter.at[pl.ds(0, prompts - 1)], send.at[1])
    landed(k_all.at[pl.ds(0, total_rows - rows)], send.at[2])
    landed(v_all.at[pl.ds(0, total_rows - rows)], send.at[3])
    landed(q_all.at[pl.ds(0, total_rows - rows)], send.at[4])
    landed(g_all.at[pl.ds(0, total_rows - rows)], send.at[5])
    landed(chosen.at[pl.ds(0, resps - 1)], send.at[6])
    landed(delta_all.at[pl.ds(0, heads - 1)], send.at[7])
    landed(dq_all.at[pl.ds(0, total_rows - rows)], send.at[8])
    landed(term_all.at[pl.ds(0, resps - 1)], send.at[9])
    landed(dk_half.at[pl.ds(0, total_rows - rows)], send.at[10])
    landed(dv_half.at[pl.ds(0, total_rows - rows)], send.at[11])
    landed(dense_all.at[pl.ds(0, prompts - 1)], send.at[12])


def on_device(
    mesh_sizes,
    queries,
    outputs,
    out_grads,
    resp_keys,
    resp_values,
    prompt_keys,
    prompt_values,
    prompt_of,
    lengths,
):
    heads, resps, prompts = mesh_sizes
    rows = queries.shape[1]
    kv_heads = resp_keys.shape[2] // HD
    group = queries.shape[2] // HD // kv_heads
    own_tokens, prompt_count = prompt_keys.shape[:2]
    total_rows = heads * rows
    stages = 4
    row_block = total_rows // 2
    span = own_tokens * prompts
    prompt_len = span * resps
    width = group * HD
    sizes = (heads, resps, prompts, group, rows, stages, row_block, own_tokens, prompt_count)

    pkv = jnp.concatenate(
        [
            prompt_keys.transpose(1, 0, 2).reshape(own_tokens * prompt_count, HD),
            prompt_values.transpose(1, 0, 2).reshape(own_tokens * prompt_count, HD),
        ],
        axis=0,
    )
    both = 2 * own_tokens * prompt_count
    vmem = pltpu.VMEM
    dma = pltpu.SemaphoreType.DMA
    hbm = pl.BlockSpec(memory_space=pl.ANY)
    smem = pl.BlockSpec(memory_space=pltpu.SMEM)
    in_vmem = pl.BlockSpec(memory_space=pltpu.VMEM)
    dq, dk, dv, dpkv = pl.pallas_call(
        functools.partial(kernel, sizes),
        out_shape=(
            jax.ShapeDtypeStruct((rows, queries.shape[2]), HALF),
            jax.ShapeDtypeStruct((rows, resp_keys.shape[2]), HALF),
            jax.ShapeDtypeStruct((rows, resp_keys.shape[2]), HALF),
            jax.ShapeDtypeStruct((both, HD), WIDE),
        ),
        in_specs=[smem, smem, hbm, hbm, hbm, hbm, hbm, in_vmem],
        out_specs=(hbm, hbm, hbm, in_vmem),
        scratch_shapes=[
            vmem((total_rows, width), HALF),
            vmem((total_rows, width), HALF),
            vmem((total_rows, HD), HALF),
            vmem((total_rows, HD), HALF),
            vmem((rows, queries.shape[2]), HALF),
            vmem((rows, queries.shape[2]), HALF),
            vmem((heads, group, 2 * rows), WIDE),
            vmem((heads, group, 2 * rows), WIDE),
            vmem((8, HD), WIDE),
            vmem((resps, 8, HD), WIDE),
            vmem((prompts, both, HD), HALF),
            vmem((resps, 2 * span, HD), HALF),
            vmem((resps, 2 * span, HD), HALF),
            vmem((HD, total_rows), HALF),
            vmem((HD, prompt_len), HALF),
            vmem((total_rows, width), HALF),
            vmem((total_rows, HD), WIDE),
            vmem((total_rows, HD), WIDE),
            vmem((prompt_len, HD), WIDE),
            vmem((prompt_len, HD), WIDE),
            vmem((total_rows, HD), HALF),
            vmem((total_rows, HD), HALF),
            vmem((resps, 2 * span, HD), HALF),
            vmem((resps, 2 * span, HD), HALF),
            vmem((prompts, both, HD), WIDE),
            vmem((prompts, both, HD), WIDE),
            dma((13,)),
            dma,
            dma,
            dma,
            dma((2,)),
            dma,
            dma((stages,)),
            dma((stages,)),
            dma,
            dma((2,)),
            dma,
            dma,
            dma((6,)),
        ],
        compiler_params=pltpu.CompilerParams(
            collective_id=0, has_side_effects=True, vmem_limit_bytes=48 * 1024 * 1024
        ),
    )(
        prompt_of,
        lengths,
        queries[0],
        outputs[0],
        out_grads[0],
        resp_keys[0],
        resp_values[0],
        pkv,
    )
    dp = dpkv.reshape(2, prompt_count, own_tokens, HD).transpose(0, 2, 1, 3).astype(HALF)
    return dq[None], dk[None], dv[None], dp[0], dp[1]


def solution(mesh):
    sizes = (mesh.shape["heads"], mesh.shape["resp"], mesh.shape["prompt"])
    return jax.shard_map(
        functools.partial(on_device, sizes),
        mesh=mesh,
        in_specs=(
            P(("resp", "prompt"), "heads", None),
            P(("resp", "prompt"), "heads", None),
            P(("resp", "prompt"), "heads", None),
            P(("resp", "prompt"), "heads", None),
            P(("resp", "prompt"), "heads", None),
            P(("resp", "prompt"), None, "heads"),
            P(("resp", "prompt"), None, "heads"),
            P(("resp", "prompt")),
            P(("resp", "prompt")),
        ),
        out_specs=(
            P(("resp", "prompt"), "heads", None),
            P(("resp", "prompt"), "heads", None),
            P(("resp", "prompt"), "heads", None),
            P(("resp", "prompt"), None, "heads"),
            P(("resp", "prompt"), None, "heads"),
        ),
        check_vma=False,
    )
```

time: 1010 us -> 75.1 us (0.07)
  the two profiles are of different devices: /device:TPU:262 before, /device:TPU:1 now
where the time goes in v1:
time: 75.1 us; the launch traced here: 74.8 us
  Pallas kernels  63.7 us (85%)
  local copies, waits for them, and re-layouts  9.09 us (12%)
  between operations  1.97 us (3%)
    pallas_call x1, Pallas kernels, on_device(): pl.pallas_call(functools.partial(kernel, sizes), out_shape=(jax.ShapeDtyp...  63.7 us
    unnamed x13, local copies, waits for them, and re-layouts  7.75 us

profile of v1, /device:TPU:1, one launch (start us, length us, event | category | flops | bytes accessed | tf_op | source)
XLA Modules:
  0.0 74.8 jit_solution(10704096906948538605)
XLA Ops:
  0.6 0.7 copy_bitcast_fusion.1
  2.7 0.0 copy-start
  2.7 1.2 %copy-done = bf16[1,64,8192]{2,1,0:T(8,128)(2,1)S(1)} copy-done((bf16[1,64,8192]{2,1,0:T(8,128)(2,1)S(1)}, bf16[1,64,8192]{2,1,0:T(8,128)(2,1)}, u32[]{:S(2)}) %copy-start) | copy-done | bytes 1048600
  3.9 0.0 copy-start.1
  3.9 1.2 %copy-done.1 = bf16[1,64,8192]{2,1,0:T(8,128)(2,1)S(1)} copy-done((bf16[1,64,8192]{2,1,0:T(8,128)(2,1)S(1)}, bf16[1,64,8192]{2,1,0:T(8,128)(2,1)}, u32[]{:S(2)}) %copy-start.1) | copy-done | bytes 1048600
  5.1 0.0 copy-start.2
  5.1 1.2 %copy-done.2 = bf16[1,64,8192]{2,1,0:T(8,128)(2,1)S(1)} copy-done((bf16[1,64,8192]{2,1,0:T(8,128)(2,1)S(1)}, bf16[1,64,8192]{2,1,0:T(8,128)(2,1)}, u32[]{:S(2)}) %copy-start.2) | copy-done | bytes 1048600
  6.3 0.0 copy-start.3
  6.3 0.9 %copy-done.3 = bf16[1,64,1024]{2,1,0:T(8,128)(2,1)S(1)} copy-done((bf16[1,64,1024]{2,1,0:T(8,128)(2,1)S(1)}, bf16[1,64,1024]{2,1,0:T(8,128)(2,1)}, u32[]{:S(2)}) %copy-start.3) | copy-done | bytes 131096
  7.2 0.0 copy-start.4
  7.2 0.9 %copy-done.4 = bf16[1,64,1024]{2,1,0:T(8,128)(2,1)S(1)} copy-done((bf16[1,64,1024]{2,1,0:T(8,128)(2,1)S(1)}, bf16[1,64,1024]{2,1,0:T(8,128)(2,1)}, u32[]{:S(2)}) %copy-start.4) | copy-done | bytes 131096
  8.1 63.7 %shard_map.128 = (bf16[64,8192]{1,0:T(8,128)(2,1)S(1)}, bf16[64,1024]{1,0:T(8,128)(2,1)S(1)}, bf16[64,1024]{1,0:T(8,128)(2,1)S(1)}, f32[64,128]{1,0:T(8,128)S(1)}) custom-call(s32[1]{0:T(128)S(6)} %copy.24.prompt_id, s32[1]{0:T(128)S(6)} %copy.25.length, bf16[64,8192]{1,0:T(8,128)(2,1)S(1)} %bitcast.22, bf16[64,8192]{1,0:T(8,128)(2,1)S(1)} %bitcast.23, ...), custom_call_target="tpu_custom_call" | custom-call | tf_op jit(solution)/shard_map/pallas_call | solution.py:417
  71.9 0.6 slice_bitcast_fusion
  72.5 1.0 %copy.26 = bf16[1,64,8192]{2,1,0:T(8,128)(2,1)} copy(bf16[1,64,8192]{2,1,0:T(8,128)(2,1)S(1)} %bitcast.25) | data formatting | bytes 2097152
  73.5 0.7 copy.27
  74.1 0.7 copy.28
  (3 shorter events, 0.0 us)
Async XLA Ops:
  2.7 1.2 %copy-start = (bf16[1,64,8192]{2,1,0:T(8,128)(2,1)S(1)}, bf16[1,64,8192]{2,1,0:T(8,128)(2,1)}, u32[]{:S(2)}) copy-start(bf16[1,64,8192]{2,1,0:T(8,128)(2,1)} %param.9) | copy-start | bytes 3145732
  3.9 1.2 %copy-start.1 = (bf16[1,64,8192]{2,1,0:T(8,128)(2,1)S(1)}, bf16[1,64,8192]{2,1,0:T(8,128)(2,1)}, u32[]{:S(2)}) copy-start(bf16[1,64,8192]{2,1,0:T(8,128)(2,1)} %param.10) | copy-start | bytes 3145732
  5.1 1.2 %copy-start.2 = (bf16[1,64,8192]{2,1,0:T(8,128)(2,1)S(1)}, bf16[1,64,8192]{2,1,0:T(8,128)(2,1)}, u32[]{:S(2)}) copy-start(bf16[1,64,8192]{2,1,0:T(8,128)(2,1)} %param.11) | copy-start | bytes 3145732
  6.3 0.9 %copy-start.3 = (bf16[1,64,1024]{2,1,0:T(8,128)(2,1)S(1)}, bf16[1,64,1024]{2,1,0:T(8,128)(2,1)}, u32[]{:S(2)}) copy-start(bf16[1,64,1024]{2,1,0:T(8,128)(2,1)} %param.12) | copy-start | bytes 393220
  7.2 0.9 %copy-start.4 = (bf16[1,64,1024]{2,1,0:T(8,128)(2,1)S(1)}, bf16[1,64,1024]{2,1,0:T(8,128)(2,1)}, u32[]{:S(2)}) copy-start(bf16[1,64,1024]{2,1,0:T(8,128)(2,1)} %param.13) | copy-start | bytes 393220

commit v2 on v1

--- a/solution.py
+++ b/solution.py
@@ -28,21 +28,27 @@
     g_in,
     k_in,
     v_in,
-    pkv_in,
+    pk_in,
+    pv_in,
     dq_out,
-    dk_out,
-    dv_out,
+    dkv_out,
     dpkv_out,
     q_all,
     g_all,
     k_all,
     v_all,
+    q_mine,
     o_mine,
     g_mine,
+    k_mine,
+    v_mine,
+    pk_mine,
+    pv_mine,
     delta_send,
     delta_all,
     id_send,
     id_all,
+    pkv_send,
     quarter,
     chosen,
     pkv_all,
@@ -104,21 +110,25 @@
 
         lax.fori_loop(1, count, step, 0)
 
-    load_o = pltpu.make_async_copy(o_in, o_mine, local.at[0])
-    load_g = pltpu.make_async_copy(g_in, g_mine, local.at[1])
-    load_o.start()
-    load_g.start()
+    loads = [
+        pltpu.make_async_copy(src, dst, local.at[n])
+        for n, (src, dst) in enumerate(
+            (
+                (pk_in, pk_mine),
+                (pv_in, pv_mine),
+                (k_in, k_mine),
+                (v_in, v_mine),
+                (q_in, q_mine),
+                (g_in, g_mine),
+                (o_in, o_mine),
+            )
+        )
+    ]
+    for copy in loads:
+        copy.start()
     own_cols = pl.ds(pl.multiple_of(me * width, width), width)
     own_rows = pl.ds(pl.multiple_of(me * rows, rows), rows)
     own_head = pl.ds(pl.multiple_of(me * HD, HD), HD)
-    keep = [
-        pltpu.make_async_copy(q_in.at[:, own_cols], q_all.at[own_rows, :], local.at[2]),
-        pltpu.make_async_copy(g_in.at[:, own_cols], g_all.at[own_rows, :], local.at[3]),
-        pltpu.make_async_copy(k_in.at[:, own_head], k_all.at[own_rows, :], local.at[4]),
-        pltpu.make_async_copy(v_in.at[:, own_head], v_all.at[own_rows, :], local.at[5]),
-    ]
-    for copy in keep:
-        copy.start()
 
     barrier = pltpu.get_barrier_semaphore()
     for axis, count, own in (("heads", heads, me), ("resp", resps, mine_r), ("prompt", prompts, mine_p)):
@@ -129,33 +139,46 @@
             )
 
         others(count, own, greet)
+    for copy in loads[:2]:
+        copy.wait()
     id_tile = jnp.full((8, HD), prompt_id[0], jnp.int32).astype(WIDE)
     id_send[...] = id_tile
     id_all[mine_r] = id_tile
-    quarter[mine_p] = pkv_in[...]
+    mine_k = pk_mine[...].astype(WIDE)
+    mine_v = pv_mine[...].astype(WIDE)
+    pkv_send[...] = jnp.concatenate(
+        [mine_k[:, c, :] for c in range(prompt_count)]
+        + [mine_v[:, c, :] for c in range(prompt_count)],
+        axis=0,
+    ).astype(HALF)
+    quarter[mine_p] = pkv_send[...]
+    for copy in loads[2:]:
+        copy.wait()
     pl.semaphore_wait(barrier, heads + resps + prompts - 3)
 
     others(resps, mine_r, lambda p: start(id_send, id_all.at[mine_r], send.at[0], recv_id, "resp", p))
     others(
         prompts,
         mine_p,
-        lambda p: start(pkv_in, quarter.at[mine_p], send.at[1], recv_quarter, "prompt", p),
+        lambda p: start(pkv_send, quarter.at[mine_p], send.at[1], recv_quarter, "prompt", p),
     )
 
     def send_kv(p):
         cols = pl.ds(pl.multiple_of(p * HD, HD), HD)
-        start(k_in.at[:, cols], k_all.at[own_rows, :], send.at[2], recv_kv.at[0], "heads", p)
-        start(v_in.at[:, cols], v_all.at[own_rows, :], send.at[3], recv_kv.at[1], "heads", p)
+        start(k_mine.at[:, cols], k_all.at[own_rows, :], send.at[2], recv_kv.at[0], "heads", p)
+        start(v_mine.at[:, cols], v_all.at[own_rows, :], send.at[3], recv_kv.at[1], "heads", p)
 
     others(heads, me, send_kv)
+    k_all[own_rows, :] = k_mine[:, own_head]
+    v_all[own_rows, :] = v_mine[:, own_head]
 
     def send_stage(stage):
         to = pl.ds(pl.multiple_of(stage * stage_width, stage_width), stage_width)
 
         def body(p):
             cols = pl.ds(pl.multiple_of(p * width + stage * stage_width, stage_width), stage_width)
-            start(q_in.at[:, cols], q_all.at[own_rows, to], send.at[4], recv_q.at[stage], "heads", p)
-            start(g_in.at[:, cols], g_all.at[own_rows, to], send.at[5], recv_g.at[stage], "heads", p)
+            start(q_mine.at[:, cols], q_all.at[own_rows, to], send.at[4], recv_q.at[stage], "heads", p)
+            start(g_mine.at[:, cols], g_all.at[own_rows, to], send.at[5], recv_g.at[stage], "heads", p)
 
         others(heads, me, body)
 
@@ -189,8 +212,8 @@
     others(resps, mine_r, send_prompt)
     pkv_all[mine_r] = choose(mine_r)
 
-    load_o.wait()
-    load_g.wait()
+    q_all[own_rows, :] = q_mine[:, own_cols]
+    g_all[own_rows, :] = g_mine[:, own_cols]
     head_of = lax.broadcasted_iota(jnp.int32, (group, width), 1) // HD
     ones = (head_of == lax.broadcasted_iota(jnp.int32, (group, width), 0)).astype(HALF)
     side = lax.rem(me, 2)
@@ -221,8 +244,6 @@
     dv_acc[...] = jnp.zeros_like(dv_acc)
     dpk_acc[...] = jnp.zeros_like(dpk_acc)
     dpv_acc[...] = jnp.zeros_like(dpv_acc)
-    for copy in keep:
-        copy.wait()
     landed(k_all.at[pl.ds(0, total_rows - rows)], recv_kv.at[0])
     landed(v_all.at[pl.ds(0, total_rows - rows)], recv_kv.at[1])
     landed(delta_all.at[pl.ds(0, heads - 1)], recv_delta)
@@ -272,9 +293,11 @@
         dq_t = dot(pkt[...], ds_p, NN) + dot(kt[:, 0:keys], ds_r, NN)
         dq_all[lo : lo + row_block, cols] = (dq_t * scale).T.astype(HALF)
 
-    def visit(stage, carry):
+    def arrive(stage):
         landed(q_all.at[pl.ds(0, total_rows - rows), pl.ds(0, stage_width)], recv_q.at[stage])
         landed(g_all.at[pl.ds(0, total_rows - rows), pl.ds(0, stage_width)], recv_g.at[stage])
+
+    def work(stage):
         for sub in range(per_stage):
             head_in_group = stage * per_stage + sub
             pick_head = (
@@ -283,6 +306,8 @@
             delta_head = jnp.sum(delta_rows * pick_head, axis=0, keepdims=True)
             for block in range(total_rows // row_block):
                 one_block(head_in_group, delta_head, block)
+
+    def give_back(stage):
         src_cols = pl.ds(pl.multiple_of(stage * stage_width, stage_width), stage_width)
         dst_cols = pl.ds(pl.multiple_of(me * width + stage * stage_width, stage_width), stage_width)
 
@@ -298,9 +323,23 @@
             )
 
         others(heads, me, give)
+
+    def visit(stage, carry):
+        arrive(stage)
+
+        @pl.when(stage == stages - 1)
+        def _():
+            def earlier(s, carry):
+                give_back(s)
+                return carry
+
+            lax.fori_loop(0, stages - 1, earlier, 0)
+
+        work(stage)
         return carry
 
     lax.fori_loop(0, stages, visit, 0)
+    give_back(stages - 1)
 
     for a in range(resps):
         lo = a * span
@@ -317,14 +356,14 @@
 
     def give_own(p):
         part_rows = pl.ds(pl.multiple_of(p * rows, rows), rows)
-        start(dk_half.at[part_rows, :], dk_out.at[:, own_head], send.at[10], recv_dkv.at[0], "heads", p)
-        start(dv_half.at[part_rows, :], dv_out.at[:, own_head], send.at[11], recv_dkv.at[1], "heads", p)
+        start(dk_half.at[part_rows, :], dkv_out.at[0, :, own_head], send.at[10], recv_dkv.at[0], "heads", p)
+        start(dv_half.at[part_rows, :], dkv_out.at[1, :, own_head], send.at[11], recv_dkv.at[1], "heads", p)
 
     others(heads, me, give_own)
     put = [
         pltpu.make_async_copy(dq_all.at[own_rows, :], dq_out.at[:, own_cols], local.at[0]),
-        pltpu.make_async_copy(dk_half.at[own_rows, :], dk_out.at[:, own_head], local.at[1]),
-        pltpu.make_async_copy(dv_half.at[own_rows, :], dv_out.at[:, own_head], local.at[2]),
+        pltpu.make_async_copy(dk_half.at[own_rows, :], dkv_out.at[0, :, own_head], local.at[1]),
+        pltpu.make_async_copy(dv_half.at[own_rows, :], dkv_out.at[1, :, own_head], local.at[2]),
     ]
     for copy in put:
         copy.start()
@@ -352,15 +391,23 @@
     result = dense_all[0]
     for b in range(1, prompts):
         result = result + dense_all[b]
-    dpkv_out[...] = result
+    for kv in range(2):
+        lo = kv * part
+        dpkv_out[kv] = jnp.stack(
+            [
+                result[lo + c * own_tokens : lo + (c + 1) * own_tokens]
+                for c in range(prompt_count)
+            ],
+            axis=1,
+        ).astype(HALF)
 
     for copy in put:
         copy.wait()
     far = pl.ds(0, (heads - 1) * width)
     far_kv = pl.ds(0, (heads - 1) * HD)
     landed(dq_out.at[:, far], recv_dq)
-    landed(dk_out.at[:, far_kv], recv_dkv.at[0])
-    landed(dv_out.at[:, far_kv], recv_dkv.at[1])
+    landed(dkv_out.at[0, :, far_kv], recv_dkv.at[0])
+    landed(dkv_out.at[1, :, far_kv], recv_dkv.at[1])
     landed(id_all.at[pl.ds(0, resps - 1)], send.at[0])
     landed(quarter.at[pl.ds(0, prompts - 1)], send.at[1])
     landed(k_all.at[pl.ds(0, total_rows - rows)], send.at[2])
@@ -401,29 +448,22 @@
     width = group * HD
     sizes = (heads, resps, prompts, group, rows, stages, row_block, own_tokens, prompt_count)
 
-    pkv = jnp.concatenate(
-        [
-            prompt_keys.transpose(1, 0, 2).reshape(own_tokens * prompt_count, HD),
-            prompt_values.transpose(1, 0, 2).reshape(own_tokens * prompt_count, HD),
-        ],
-        axis=0,
-    )
     both = 2 * own_tokens * prompt_count
     vmem = pltpu.VMEM
     dma = pltpu.SemaphoreType.DMA
+    in_hbm = functools.partial(pltpu.with_memory_space_constraint, memory_space=pltpu.HBM)
     hbm = pl.BlockSpec(memory_space=pl.ANY)
     smem = pl.BlockSpec(memory_space=pltpu.SMEM)
     in_vmem = pl.BlockSpec(memory_space=pltpu.VMEM)
-    dq, dk, dv, dpkv = pl.pallas_call(
+    dq, dkv, dpkv = pl.pallas_call(
         functools.partial(kernel, sizes),
         out_shape=(
             jax.ShapeDtypeStruct((rows, queries.shape[2]), HALF),
-            jax.ShapeDtypeStruct((rows, resp_keys.shape[2]), HALF),
-            jax.ShapeDtypeStruct((rows, resp_keys.shape[2]), HALF),
-            jax.ShapeDtypeStruct((both, HD), WIDE),
+            jax.ShapeDtypeStruct((2, rows, resp_keys.shape[2]), HALF),
+            jax.ShapeDtypeStruct((2, own_tokens, prompt_count, HD), HALF),
         ),
-        in_specs=[smem, smem, hbm, hbm, hbm, hbm, hbm, in_vmem],
-        out_specs=(hbm, hbm, hbm, in_vmem),
+        in_specs=[smem] * 2 + [hbm] * 7,
+        out_specs=(hbm, hbm, in_vmem),
         scratch_shapes=[
             vmem((total_rows, width), HALF),
             vmem((total_rows, width), HALF),
@@ -431,10 +471,16 @@
             vmem((total_rows, HD), HALF),
             vmem((rows, queries.shape[2]), HALF),
             vmem((rows, queries.shape[2]), HALF),
+            vmem((rows, queries.shape[2]), HALF),
+            vmem((rows, resp_keys.shape[2]), HALF),
+            vmem((rows, resp_keys.shape[2]), HALF),
+            vmem((own_tokens, prompt_count, HD), HALF),
+            vmem((own_tokens, prompt_count, HD), HALF),
             vmem((heads, group, 2 * rows), WIDE),
             vmem((heads, group, 2 * rows), WIDE),
             vmem((8, HD), WIDE),
             vmem((resps, 8, HD), WIDE),
+            vmem((both, HD), HALF),
             vmem((prompts, both, HD), HALF),
             vmem((resps, 2 * span, HD), HALF),
             vmem((resps, 2 * span, HD), HALF),
@@ -463,7 +509,7 @@
             dma((2,)),
             dma,
             dma,
-            dma((6,)),
+            dma((7,)),
         ],
         compiler_params=pltpu.CompilerParams(
             collective_id=0, has_side_effects=True, vmem_limit_bytes=48 * 1024 * 1024
@@ -471,15 +517,15 @@
     )(
         prompt_of,
         lengths,
-        queries[0],
-        outputs[0],
-        out_grads[0],
-        resp_keys[0],
-        resp_values[0],
-        pkv,
-    )
-    dp = dpkv.reshape(2, prompt_count, own_tokens, HD).transpose(0, 2, 1, 3).astype(HALF)
-    return dq[None], dk[None], dv[None], dp[0], dp[1]
+        in_hbm(queries[0]),
+        in_hbm(outputs[0]),
+        in_hbm(out_grads[0]),
+        in_hbm(resp_keys[0]),
+        in_hbm(resp_values[0]),
+        in_hbm(prompt_keys),
+        in_hbm(prompt_values),
+    )
+    return dq[None], dkv[0][None], dkv[1][None], dpkv[0], dpkv[1]
 
 
 def solution(mesh):

time: 75.1 us -> 66.4 us (0.88)
  local copies, waits for them, and re-layouts: 9.09 us -> 2.29 us
  Pallas kernels: 63.7 us -> 62 us
    unnamed x13 -> x1, local copies, waits for them, and re-layouts: 7.75 us -> 0.97 us
    pallas_call x1, Pallas kernels: 63.7 us -> 62 us  [on_device(): pl.pallas_call(functools.partial(kernel, sizes), out_shape=(jax.ShapeDtyp...]
where the time goes in v2:
time: 66.4 us; the launch traced here: 66.3 us
  Pallas kernels  62 us (93%)
  local copies, waits for them, and re-layouts  2.29 us (3%)
  between operations  1.94 us (3%)
    pallas_call x1, Pallas kernels, on_device(): pl.pallas_call(functools.partial(kernel, sizes), out_shape=(jax.ShapeDtyp...  62 us

profile of v2, /device:TPU:1, one launch (start us, length us, event | category | flops | bytes accessed | tf_op | source)
XLA Modules:
  0.0 66.3 jit_solution(17601837156293906306)
XLA Ops:
  1.9 62.0 %shard_map.128 = (bf16[64,8192]{1,0:T(8,128)(2,1)S(1)}, bf16[2,64,1024]{2,1,0:T(8,128)(2,1)S(1)}, bf16[2,8,4,128]{3,2,1,0:T(4,128)(2,1)S(1)}) custom-call(s32[1]{0:T(128)S(6)} %copy.15.prompt_id, s32[1]{0:T(128)S(6)} %copy.16.length, bf16[64,8192]{1,0:T(8,128)(2,1)} %bitcast.11, bf16[64,8192]{1,0:T(8,128)(2,1)} %bitcast.12, bf16[64,8192]{1,0:T(8,128)(2,1)} %bitcast.13, ...), custom_call_target="tpu_custom_call" | custom-call | tf_op jit(solution)/shard_map/pallas_call | solution.py:458
  64.0 0.6 slice_bitcast_fusion
  64.6 0.7 %fusion = (bf16[1,64,1024]{2,1,0:T(8,128)(2,1)}, bf16[1,64,1024]{2,1,0:T(8,128)(2,1)}) fusion(bf16[2,64,1024]{2,1,0:T(8,128)(2,1)S(1)} %get-tuple-element.9), kind=kLoop, calls=%fused_computation.2 | loop fusion | bytes 524288 | tf_op jit(solution)/shard_map/slice | solution.py:528
  65.3 1.0 %copy.17 = bf16[1,64,8192]{2,1,0:T(8,128)(2,1)} copy(bf16[1,64,8192]{2,1,0:T(8,128)(2,1)S(1)} %bitcast.10) | data formatting | bytes 2097152

commit v3 on v2

v3 whole, which is shorter than its diff:
```python
import functools

import jax
import jax.numpy as jnp
from jax import lax
from jax.experimental import pallas as pl
from jax.experimental.pallas import tpu as pltpu
from jax.sharding import PartitionSpec as P

HD = 128
LOG2E = 1.4426950408889634
WIDE = jnp.float32
HALF = jnp.bfloat16
NT = (((1,), (1,)), ((), ()))
NN = (((1,), (0,)), ((), ()))


def dot(a, b, dims):
    return lax.dot_general(a, b, dims, preferred_element_type=WIDE)


def kernel(
    sizes,
    prompt_id,
    length,
    q_in,
    o_in,
    g_in,
    k_in,
    v_in,
    pk_in,
    pv_in,
    dq_out,
    dkv_out,
    dpkv_out,
    qg_mine,
    o_mine,
    kv_mine,
    p_mine,
    qg_all,
    qg_far,
    kv_all,
    delta_send,
    delta_all,
    delta_far,
    id_send,
    id_all,
    packed,
    quarter,
    chosen,
    pkv_all,
    kt,
    pkt,
    dq_all,
    dq_far,
    dkv_acc,
    dp_acc,
    dkv_half,
    dkv_land,
    term_send,
    term_all,
    dense,
    dense_all,
    send,
    recv_id,
    recv_quarter,
    recv_pkv,
    recv_kv,
    recv_delta,
    recv_delta_far,
    recv_qg,
    recv_qg_far,
    recv_dq,
    recv_dq_far,
    recv_dkv,
    recv_term,
    recv_dense,
    local,
):
    heads, resps, prompts, group, rows, stages, own_tokens, prompt_count = sizes
    chips = heads // 2
    me = lax.axis_index("heads")
    chip, core = me // 2, lax.rem(me, 2)
    sibling = me + 1 - 2 * core
    far = lax.rem(me + chips, heads)
    far_chip = far // 2
    far_sibling = lax.rem(sibling + chips, heads)
    mine_r = lax.axis_index("resp")
    mine_p = lax.axis_index("prompt")
    chip_rows = 2 * rows
    total_rows = heads * rows
    width = group * HD
    per_stage = group // stages
    stage_width = per_stage * HD
    span = own_tokens * prompts
    prompt_len = resps * span
    part = prompt_count * own_tokens
    near = [
        (offset, side) for offset in range(1, chips) if 2 * offset != chips for side in (0, 1)
    ]
    n_near = len(near) + 1
    scale = HD**-0.5

    def start(src, dst, send_sem, recv_sem, axis, index):
        device = index if axis is None else {axis: index}
        pltpu.make_async_remote_copy(
            src_ref=src,
            dst_ref=dst,
            send_sem=send_sem,
            recv_sem=recv_sem,
            device_id=device,
            device_id_type=pl.DeviceIdType.MESH,
        ).start()

    def landed(ref, sem):
        pltpu.make_async_copy(ref, ref, sem).wait()

    def others(count, own, body):
        def step(i, carry):
            body(lax.rem(own + i, count))
            return carry

        lax.fori_loop(1, count, step, 0)

    def neighbours(body):
        for offset, side in near:
            body(lax.rem(chip + offset, chips) * 2 + side)
        body(sibling)

    def span_of(index, size):
        return pl.ds(pl.multiple_of(index * size, size), size)

    loads = [
        pltpu.make_async_copy(src, dst, local.at[n])
        for n, (src, dst) in enumerate(
            (
                (pk_in, p_mine.at[0]),
                (pv_in, p_mine.at[1]),
                (k_in, kv_mine.at[0]),
                (v_in, kv_mine.at[1]),
                (q_in, qg_mine.at[0]),
                (g_in, qg_mine.at[1]),
                (o_in, o_mine),
            )
        )
    ]
    for copy in loads:
        copy.start()
    own_rows = span_of(me, rows)
    side_rows = span_of(core, rows)

    delta_all[...] = jnp.zeros_like(delta_all)
    dkv_land[...] = jnp.zeros_like(dkv_land)
    barrier = pltpu.get_barrier_semaphore()
    for axis, count, own in (("heads", heads, me), ("resp", resps, mine_r), ("prompt", prompts, mine_p)):

        def greet(peer, axis=axis):
            pl.semaphore_signal(
                barrier, inc=1, device_id={axis: peer}, device_id_type=pl.DeviceIdType.MESH
            )

        others(count, own, greet)
    others(
        prompts,
        mine_p,
        lambda p: pl.semaphore_signal(
            barrier,
            inc=1,
            device_id={"heads": far, "prompt": p},
            device_id_type=pl.DeviceIdType.MESH,
        ),
    )
    for copy in loads[:2]:
        copy.wait()
    id_tile = jnp.full((8, HD), prompt_id[0], jnp.int32).astype(WIDE)
    id_send[...] = id_tile
    id_all[mine_r] = id_tile
    mine_k = p_mine[0].astype(WIDE)
    mine_v = p_mine[1].astype(WIDE)
    packed[...] = jnp.concatenate(
        [mine_k[:, c, :] for c in range(prompt_count)]
        + [mine_v[:, c, :] for c in range(prompt_count)],
        axis=0,
    ).astype(HALF)
    quarter[0, mine_p] = packed[...]
    for copy in loads[2:]:
        copy.wait()
    pl.semaphore_wait(barrier, heads + resps + 2 * prompts - 4)

    others(resps, mine_r, lambda p: start(id_send, id_all.at[mine_r], send.at[3], recv_id, "resp", p))
    others(
        prompts,
        mine_p,
        lambda p: start(packed, quarter.at[0, mine_p], send.at[0], recv_quarter.at[0], "prompt", p),
    )
    for offset in range(prompts):
        start(
            packed,
            quarter.at[1, mine_p],
            send.at[1],
            recv_quarter.at[1],
            None,
            {"heads": far, "prompt": lax.rem(mine_p + offset, prompts)},
        )

    def kv_cols(g, index):
        return span_of(index if g == 0 else lax.rem(index + chips, heads), HD)

    def send_kv(g):
        def body(p):
            def go():
                start(
                    kv_mine.at[:, :, kv_cols(g, p)],
                    kv_all.at[g, :, own_rows, :],
                    send.at[4 + g],
                    recv_kv.at[g],
                    "heads",
                    p,
                )

            if g == 0:
                go()
            else:
                pl.when(chip <= p // 2)(go)

        others(heads, me, body)
        kv_all[g, :, own_rows, :] = kv_mine[:, :, kv_cols(g, me)]

    send_kv(0)

    def send_stage(stage):
        to = span_of(stage, stage_width)

        def body(p):
            cols = pl.ds(pl.multiple_of(p * width + stage * stage_width, stage_width), stage_width)
            start(
                qg_mine.at[:, :, cols],
                qg_all.at[:, own_rows, to],
                send.at[6],
                recv_qg.at[stage],
                "heads",
                p,
            )

        neighbours(body)

    qg_far[:, side_rows, :] = qg_mine[:, :, span_of(far, width)]
    qg_all[:, own_rows, :] = qg_mine[:, :, span_of(me, width)]

    def weights(index):
        return [(id_all[index] == float(c)).astype(WIDE)[0:1] for c in range(prompt_count)]

    def choose_and_send(g):
        landed(quarter.at[g, pl.ds(0, prompts - 1 + g)], recv_quarter.at[g])
        held = [quarter[g, b].astype(WIDE) for b in range(prompts)]

        def pick(kv, c):
            lo = kv * part + c * own_tokens
            return jnp.concatenate([h[lo : lo + own_tokens] for h in held], axis=0)

        by_prompt = [jnp.concatenate([pick(0, c), pick(1, c)], axis=0) for c in range(prompt_count)]

        def choose(p):
            w = weights(p)
            out = w[0] * by_prompt[0]
            for c in range(1, prompt_count):
                out = out + w[c] * by_prompt[c]
            return out.astype(HALF)

        for a in range(resps):
            chosen[g, a] = choose(a)
        others(
            resps,
            mine_r,
            lambda p: start(
                chosen.at[g, p], pkv_all.at[g, mine_r], send.at[8 + g], recv_pkv.at[g], "resp", p
            ),
        )
        pkv_all[g, mine_r] = chosen[g, mine_r]

    landed(id_all.at[pl.ds(0, resps - 1)], recv_id)
    choose_and_send(0)
    send_stage(0)
    start(
        qg_mine.at[:, :, span_of(far_sibling, width)],
        qg_far.at[:, side_rows, :],
        send.at[7],
        recv_qg_far,
        "heads",
        sibling,
    )
    choose_and_send(1)
    send_stage(1)

    head_of = lax.broadcasted_iota(jnp.int32, (group, width), 1) // HD
    ones = (head_of == lax.broadcasted_iota(jnp.int32, (group, width), 0)).astype(HALF)
    first = (lax.broadcasted_iota(jnp.int32, (group, chip_rows), 1) // rows) == core

    def delta_for(p):
        cols = slice(p * width, (p + 1) * width)
        prod = o_mine[:, cols].astype(WIDE) * qg_mine[1, :, cols].astype(WIDE)
        high = prod.astype(HALF)
        low = (prod - high.astype(WIDE)).astype(HALF)
        d = dot(ones, high, NT) + dot(ones, low, NT)
        return jnp.where(first, jnp.concatenate([d, d], axis=1), 0.0)

    for p in range(heads):
        delta_send[p] = delta_for(p)
    neighbours(
        lambda p: start(delta_send.at[p], delta_all.at[me], send.at[10], recv_delta, "heads", p)
    )
    start(delta_send.at[far_sibling], delta_far.at[core], send.at[11], recv_delta_far, "heads", sibling)
    delta_all[me] = delta_send[me]
    delta_far[core] = delta_send[far]

    send_kv(1)

    def rest(stage, carry):
        send_stage(stage)
        return carry

    lax.fori_loop(2, stages, rest, 0)

    dkv_acc[...] = jnp.zeros_like(dkv_acc)
    dp_acc[...] = jnp.zeros_like(dp_acc)
    live = (lax.broadcasted_iota(jnp.int32, (1, total_rows), 1) < length[0]).astype(WIDE)
    lanes = per_stage * chip_rows
    causal = lax.broadcasted_iota(jnp.int32, (chip_rows, lanes), 0) <= lax.rem(
        lax.broadcasted_iota(jnp.int32, (chip_rows, lanes), 1), chip_rows
    )

    def transposed(g):
        kt[g] = kv_all[g, 0].T
        pkt[g] = pkv_all[g, :, 0:span, :].reshape(prompt_len, HD).T

    def blocks(g, work):
        pk = pkv_all[g, :, 0:span, :].reshape(prompt_len, HD)
        pv = pkv_all[g, :, span : 2 * span, :].reshape(prompt_len, HD)
        probs_p, probs_r, dscores_p, dscores_r = [], [], [], []
        for k, q, grad, d in work:
            lo = k * chip_rows
            keys = lo + chip_rows
            score_p = dot(pk, q, NT)
            score_r = dot(kv_all[g, 0, 0:keys, :], q, NT)
            diag = jnp.where(causal, score_r[lo:keys], -jnp.inf)
            score_r = diag if lo == 0 else jnp.concatenate([score_r[0:lo], diag], axis=0)
            peak = jnp.maximum(
                jnp.max(score_p, axis=0, keepdims=True), jnp.max(score_r, axis=0, keepdims=True)
            )
            e_p = jnp.exp2((score_p - peak) * (scale * LOG2E))
            e_r = jnp.exp2((score_r - peak) * (scale * LOG2E))
            total = jnp.sum(e_p, axis=0, keepdims=True) + jnp.sum(e_r, axis=0, keepdims=True)
            norm = jnp.concatenate([live[:, lo:keys]] * per_stage, axis=1) / total
            prob_p = e_p * norm
            prob_r = e_r * norm
            dscores_p.append((prob_p * (dot(pv, grad, NT) - d)).astype(HALF))
            dscores_r.append((prob_r * (dot(kv_all[g, 1, 0:keys, :], grad, NT) - d)).astype(HALF))
            probs_p.append(prob_p.astype(HALF))
            probs_r.append(prob_r.astype(HALF))
        every_q = jnp.concatenate([w[1] for w in work], axis=0)
        every_grad = jnp.concatenate([w[2] for w in work], axis=0)
        dp_acc[g, 1] += dot(jnp.concatenate(probs_p, axis=1), every_grad, NN)
        dp_acc[g, 0] += dot(jnp.concatenate(dscores_p, axis=1), every_q, NN)
        dqs = []
        for n, (k, q, grad, d) in enumerate(work):
            keys = (k + 1) * chip_rows
            dkv_acc[g, 1, 0:keys, :] += dot(probs_r[n], grad, NN)
            dkv_acc[g, 0, 0:keys, :] += dot(dscores_r[n], q, NN)
            dq_t = dot(pkt[g], dscores_p[n], NN) + dot(kt[g, :, 0:keys], dscores_r[n], NN)
            dqs.append((dq_t * scale).T.astype(HALF))
        return dqs

    def head_cols(stage, sub):
        return span_of(stage * per_stage + sub, HD)

    def delta_of(table, stage, lo):
        size = table.shape[1]
        out = []
        for sub in range(per_stage):
            mask = (
                lax.broadcasted_iota(jnp.int32, (group, size), 0) == stage * per_stage + sub
            ).astype(WIDE)
            out.append(jnp.sum(table * mask, axis=0, keepdims=True)[:, lo : lo + chip_rows])
        return jnp.concatenate(out, axis=1)

    def stacked(ref, kind, at, stage):
        return jnp.concatenate(
            [ref[kind, at, head_cols(stage, sub)] for sub in range(per_stage)], axis=0
        )

    def far_work():
        table = delta_far[0] + delta_far[1]
        every = slice(0, chip_rows)

        def visit(pair, carry):
            for k in range(chips):

                @pl.when(chip == k)
                def _(k=k):
                    both = [2 * pair, 2 * pair + 1]
                    dqs = blocks(
                        1,
                        [
                            (
                                k,
                                stacked(qg_far, 0, every, stage),
                                stacked(qg_far, 1, every, stage),
                                delta_of(table, stage, 0),
                            )
                            for stage in both
                        ],
                    )
                    for stage, dq in zip(both, dqs):
                        for sub in range(per_stage):
                            dq_far[:, head_cols(stage, sub)] = dq[
                                sub * chip_rows : (sub + 1) * chip_rows
                            ]

            return carry

        lax.fori_loop(0, stages // 2, visit, 0)

    def give_dkv(g):
        dkv_half[g, 0] = (dkv_acc[g, 0] * scale).astype(HALF)
        dkv_half[g, 1] = dkv_acc[g, 1].astype(HALF)
        cols = kv_cols(g, me)

        def body(p):
            def go():
                start(
                    dkv_half.at[g, :, span_of(p, rows), :],
                    dkv_land.at[g, :, :, cols],
                    send.at[12 + g],
                    recv_dkv.at[g],
                    "heads",
                    p,
                )

            if g == 0:
                go()
            else:
                pl.when(p // 2 <= chip)(go)

        others(heads, me, body)
        dkv_land[g, :, :, cols] = dkv_half[g, :, own_rows, :]

    def send_terms(g):
        for a in range(resps):
            lo = a * span
            term_send[g, a] = jnp.concatenate(
                [dp_acc[g, 0, lo : lo + span, :] * scale, dp_acc[g, 1, lo : lo + span, :]], axis=0
            ).astype(HALF)
        others(
            resps,
            mine_r,
            lambda p: start(
                term_send.at[g, p], term_all.at[g, mine_r], send.at[14 + g], recv_term.at[g], "resp", p
            ),
        )
        term_all[g, mine_r] = term_send[g, mine_r]

    def send_dense(g):
        landed(term_all.at[g, pl.ds(0, resps - 1)], recv_term.at[g])

        def add(a, sums):
            w = weights(a)
            term = term_all[g, a].astype(WIDE)
            return tuple(s + w[c] * term for c, s in enumerate(sums))

        sums = lax.fori_loop(
            0, resps, add, tuple(jnp.zeros((2 * span, HD), WIDE) for c in range(prompt_count))
        )
        for b in range(prompts):
            pieces = []
            for kv in range(2):
                for c in range(prompt_count):
                    lo = kv * span + b * own_tokens
                    pieces.append(sums[c][lo : lo + own_tokens])
            dense[g, b] = jnp.concatenate(pieces, axis=0)
        if g == 0:
            dense_all[0, mine_p] = dense[0, mine_p]
        for offset in range(1 - g, prompts):
            p = lax.rem(mine_p + offset, prompts)
            start(
                dense.at[g, p],
                dense_all.at[g, mine_p],
                send.at[16 + g],
                recv_dense.at[g],
                None,
                {"heads": me if g == 0 else far, "prompt": p},
            )

    landed(kv_all.at[0, :, pl.ds(0, total_rows - rows), :], recv_kv.at[0])
    landed(delta_all.at[pl.ds(0, n_near)], recv_delta)
    landed(pkv_all.at[0, pl.ds(0, resps - 1)], recv_pkv.at[0])
    transposed(0)
    delta_rows = jnp.concatenate(
        [delta_all[2 * k] + delta_all[2 * k + 1] for k in range(chips)], axis=1
    )

    def give_back(stage):
        src_cols = span_of(stage, stage_width)
        dst_cols = pl.ds(pl.multiple_of(me * width + stage * stage_width, stage_width), stage_width)
        neighbours(
            lambda p: start(
                dq_all.at[span_of(p, rows), src_cols],
                dq_out.at[:, dst_cols],
                send.at[18],
                recv_dq,
                "heads",
                p,
            )
        )

    def visit(stage, carry):
        landed(qg_all.at[:, pl.ds(0, n_near * rows), pl.ds(0, stage_width)], recv_qg.at[stage])
        for away in range(chips):

            @pl.when(far_chip == away)
            def _(away=away):
                chosen_chips = [k for k in range(chips) if k != away]
                places = [slice(k * chip_rows, (k + 1) * chip_rows) for k in chosen_chips]
                dqs = blocks(
                    0,
                    [
                        (
                            k,
                            stacked(qg_all, 0, at, stage),
                            stacked(qg_all, 1, at, stage),
                            delta_of(delta_rows, stage, k * chip_rows),
                        )
                        for k, at in zip(chosen_chips, places)
                    ],
                )
                for at, dq in zip(places, dqs):
                    for sub in range(per_stage):
                        dq_all[at, head_cols(stage, sub)] = dq[
                            sub * chip_rows : (sub + 1) * chip_rows
                        ]

        @pl.when(stage < stages - 1)
        def _():
            give_back(stage)

        @pl.when(stage == 0)
        def _():
            for k in range(chips):

                @pl.when(chip == k)
                def _(k=k):
                    landed(kv_all.at[1, :, pl.ds(0, (2 * k + 1) * rows), :], recv_kv.at[1])

            landed(delta_far.at[0], recv_delta_far)
            landed(qg_far.at[:, pl.ds(0, rows), :], recv_qg_far)
            landed(pkv_all.at[1, pl.ds(0, resps - 1)], recv_pkv.at[1])
            transposed(1)
            far_work()
            start(
                dq_far.at[span_of(1 - core, rows), :],
                dq_out.at[:, span_of(far, width)],
                send.at[19],
                recv_dq_far,
                "heads",
                sibling,
            )
            send_terms(1)
            give_dkv(1)

        return carry

    lax.fori_loop(0, stages, visit, 0)

    send_terms(0)
    give_back(stages - 1)
    give_dkv(0)
    put = [
        pltpu.make_async_copy(
            dq_all.at[own_rows, :], dq_out.at[:, span_of(me, width)], local.at[0]
        ),
        pltpu.make_async_copy(
            dq_far.at[side_rows, :], dq_out.at[:, span_of(far, width)], local.at[1]
        ),
    ]
    for copy in put:
        copy.start()
    send_dense(1)
    send_dense(0)
    for g in range(2):
        landed(dense_all.at[g, pl.ds(0, prompts - 1 + g)], recv_dense.at[g])
    result = dense_all[0, 0]
    for b in range(1, prompts):
        result = result + dense_all[0, b]
    for b in range(prompts):
        result = result + dense_all[1, b]
    for kv in range(2):
        lo = kv * part
        dpkv_out[kv] = jnp.stack(
            [
                result[lo + c * own_tokens : lo + (c + 1) * own_tokens]
                for c in range(prompt_count)
            ],
            axis=1,
        ).astype(HALF)

    landed(dkv_land.at[0, :, :, pl.ds(0, (heads - 1) * HD)], recv_dkv.at[0])
    for k in range(chips):

        @pl.when(chip == k)
        def _(k=k):
            from_later = 2 * (chips - k) - 1
            landed(dkv_land.at[1, :, :, pl.ds(0, from_later * HD)], recv_dkv.at[1])
            landed(kv_all.at[1, :, pl.ds(0, from_later * rows), :], send.at[5])
            landed(kv_all.at[1, :, pl.ds(0, (2 * k + 1) * rows), :], send.at[13])

    for kv in range(2):
        dkv_out[kv] = (dkv_land[0, kv].astype(WIDE) + dkv_land[1, kv].astype(WIDE)).astype(HALF)

    for copy in put:
        copy.wait()
    landed(dq_out.at[:, pl.ds(0, n_near * width)], recv_dq)
    landed(dq_out.at[:, pl.ds(0, width)], recv_dq_far)
    for g in range(2):
        landed(quarter.at[g, pl.ds(0, prompts - 1 + g)], send.at[g])
        landed(chosen.at[g, pl.ds(0, resps - 1)], send.at[8 + g])
        landed(term_all.at[g, pl.ds(0, resps - 1)], send.at[14 + g])
        landed(dense_all.at[g, pl.ds(0, prompts - 1 + g)], send.at[16 + g])
    landed(id_all.at[pl.ds(0, resps - 1)], send.at[3])
    landed(kv_all.at[0, :, pl.ds(0, total_rows - rows), :], send.at[4])
    landed(qg_all.at[:, pl.ds(0, n_near * rows), :], send.at[6])
    landed(qg_far.at[:, pl.ds(0, rows), :], send.at[7])
    landed(delta_all.at[pl.ds(0, n_near)], send.at[10])
    landed(delta_far.at[0], send.at[11])
    landed(dkv_half.at[0, :, pl.ds(0, total_rows - rows), :], send.at[12])
    landed(dq_all.at[pl.ds(0, n_near * rows), :], send.at[18])
    landed(dq_far.at[pl.ds(0, rows), :], send.at[19])


def on_device(
    mesh_sizes,
    queries,
    outputs,
    out_grads,
    resp_keys,
    resp_values,
    prompt_keys,
    prompt_values,
    prompt_of,
    lengths,
):
    heads, resps, prompts = mesh_sizes
    rows = queries.shape[1]
    kv_heads = resp_keys.shape[2] // HD
    group = queries.shape[2] // HD // kv_heads
    own_tokens, prompt_count = prompt_keys.shape[:2]
    total_rows = heads * rows
    stages = 4
    span = own_tokens * prompts
    prompt_len = span * resps
    width = group * HD
    sizes = (heads, resps, prompts, group, rows, stages, own_tokens, prompt_count)
    columns = queries.shape[2]
    kv_columns = resp_keys.shape[2]
    chip_rows = 2 * rows
    both = 2 * own_tokens * prompt_count
    vmem = pltpu.VMEM
    dma = pltpu.SemaphoreType.DMA
    in_hbm = functools.partial(pltpu.with_memory_space_constraint, memory_space=pltpu.HBM)
    hbm = pl.BlockSpec(memory_space=pl.ANY)
    smem = pl.BlockSpec(memory_space=pltpu.SMEM)
    in_vmem = pl.BlockSpec(memory_space=pltpu.VMEM)
    dq, dkv, dpkv = pl.pallas_call(
        functools.partial(kernel, sizes),
        out_shape=(
            jax.ShapeDtypeStruct((rows, queries.shape[2]), HALF),
            jax.ShapeDtypeStruct((2, rows, resp_keys.shape[2]), HALF),
            jax.ShapeDtypeStruct((2, own_tokens, prompt_count, HD), HALF),
        ),
        in_specs=[smem] * 2 + [hbm] * 7,
        out_specs=(hbm, in_vmem, in_vmem),
        scratch_shapes=[
            vmem((2, rows, columns), HALF),
            vmem((rows, columns), HALF),
            vmem((2, rows, kv_columns), HALF),
            vmem((2, own_tokens, prompt_count, HD), HALF),
            vmem((2, total_rows, width), HALF),
            vmem((2, chip_rows, width), HALF),
            vmem((2, 2, total_rows, HD), HALF),
            vmem((heads, group, chip_rows), WIDE),
            vmem((heads, group, chip_rows), WIDE),
            vmem((2, group, chip_rows), WIDE),
            vmem((8, HD), WIDE),
            vmem((resps, 8, HD), WIDE),
            vmem((both, HD), HALF),
            vmem((2, prompts, both, HD), HALF),
            vmem((2, resps, 2 * span, HD), HALF),
            vmem((2, resps, 2 * span, HD), HALF),
            vmem((2, HD, total_rows), HALF),
            vmem((2, HD, prompt_len), HALF),
            vmem((total_rows, width), HALF),
            vmem((chip_rows, width), HALF),
            vmem((2, 2, total_rows, HD), WIDE),
            vmem((2, 2, prompt_len, HD), WIDE),
            vmem((2, 2, total_rows, HD), HALF),
            vmem((2, 2, rows, kv_columns), HALF),
            vmem((2, resps, 2 * span, HD), HALF),
            vmem((2, resps, 2 * span, HD), HALF),
            vmem((2, prompts, both, HD), WIDE),
            vmem((2, prompts, both, HD), WIDE),
            dma((20,)),
            dma,
            dma((2,)),
            dma((2,)),
            dma((2,)),
            dma,
            dma,
            dma((stages,)),
            dma,
            dma,
            dma,
            dma((2,)),
            dma((2,)),
            dma((2,)),
            dma((7,)),
        ],
        compiler_params=pltpu.CompilerParams(
            collective_id=0, has_side_effects=True, vmem_limit_bytes=48 * 1024 * 1024
        ),
    )(
        prompt_of,
        lengths,
        in_hbm(queries[0]),
        in_hbm(outputs[0]),
        in_hbm(out_grads[0]),
        in_hbm(resp_keys[0]),
        in_hbm(resp_values[0]),
        in_hbm(prompt_keys),
        in_hbm(prompt_values),
    )
    return dq[None], dkv[0][None], dkv[1][None], dpkv[0], dpkv[1]


def solution(mesh):
    sizes = (mesh.shape["heads"], mesh.shape["resp"], mesh.shape["prompt"])
    return jax.shard_map(
        functools.partial(on_device, sizes),
        mesh=mesh,
        in_specs=(
            P(("resp", "prompt"), "heads", None),
            P(("resp", "prompt"), "heads", None),
            P(("resp", "prompt"), "heads", None),
            P(("resp", "prompt"), "heads", None),
            P(("resp", "prompt"), "heads", None),
            P(("resp", "prompt"), None, "heads"),
            P(("resp", "prompt"), None, "heads"),
            P(("resp", "prompt")),
            P(("resp", "prompt")),
        ),
        out_specs=(
            P(("resp", "prompt"), "heads", None),
            P(("resp", "prompt"), "heads", None),
            P(("resp", "prompt"), "heads", None),
            P(("resp", "prompt"), None, "heads"),
            P(("resp", "prompt"), None, "heads"),
        ),
        check_vma=False,
    )
```

time: 66.4 us -> 68 us (1.024)
  the two profiles are of different devices: /device:TPU:1 before, /device:TPU:4 now
where the time goes in v3:
time: 68 us; the launch traced here: 67.8 us
  Pallas kernels  63.6 us (94%)
  local copies, waits for them, and re-layouts  2.29 us (3%)
  between operations  1.94 us (3%)
    pallas_call x1, Pallas kernels, on_device(): pl.pallas_call(functools.partial(kernel, sizes), out_shape=(jax.ShapeDtyp...  63.6 us

profile of v3, /device:TPU:4, one launch (start us, length us, event | category | flops | bytes accessed | tf_op | source)
XLA Modules:
  0.0 67.8 jit_solution(14563758788894229788)
XLA Ops:
  1.9 63.6 %shard_map.128 = (bf16[64,8192]{1,0:T(8,128)(2,1)S(1)}, bf16[2,64,1024]{2,1,0:T(8,128)(2,1)S(1)}, bf16[2,8,4,128]{3,2,1,0:T(4,128)(2,1)S(1)}) custom-call(s32[1]{0:T(128)S(6)} %copy.15.prompt_id, s32[1]{0:T(128)S(6)} %copy.16.length, bf16[64,8192]{1,0:T(8,128)(2,1)} %bitcast.11, bf16[64,8192]{1,0:T(8,128)(2,1)} %bitcast.12, bf16[64,8192]{1,0:T(8,128)(2,1)} %bitcast.13, ...), custom_call_target="tpu_custom_call" | custom-call | tf_op jit(solution)/shard_map/pallas_call | solution.py:671
  65.5 0.6 slice_bitcast_fusion
  66.1 0.7 %fusion = (bf16[1,64,1024]{2,1,0:T(8,128)(2,1)}, bf16[1,64,1024]{2,1,0:T(8,128)(2,1)}) fusion(bf16[2,64,1024]{2,1,0:T(8,128)(2,1)S(1)} %get-tuple-element.9), kind=kLoop, calls=%fused_computation.2 | loop fusion | bytes 524288 | tf_op jit(solution)/shard_map/slice | solution.py:739
  66.9 1.0 %copy.17 = bf16[1,64,8192]{2,1,0:T(8,128)(2,1)} copy(bf16[1,64,8192]{2,1,0:T(8,128)(2,1)S(1)} %bitcast.10) | data formatting | bytes 2097152

commit v4 on v2

--- a/solution.py
+++ b/solution.py
@@ -341,6 +341,15 @@
     lax.fori_loop(0, stages, visit, 0)
     give_back(stages - 1)
 
+    dk_half[...] = (dk_acc[...] * scale).astype(HALF)
+    dv_half[...] = dv_acc[...].astype(HALF)
+
+    def give_own(p):
+        part_rows = pl.ds(pl.multiple_of(p * rows, rows), rows)
+        start(dk_half.at[part_rows, :], dkv_out.at[0, :, own_head], send.at[10], recv_dkv.at[0], "heads", p)
+        start(dv_half.at[part_rows, :], dkv_out.at[1, :, own_head], send.at[11], recv_dkv.at[1], "heads", p)
+
+    others(heads, me, give_own)
     for a in range(resps):
         lo = a * span
         term_send[a] = jnp.concatenate(
@@ -351,15 +360,6 @@
         mine_r,
         lambda p: start(term_send.at[p], term_all.at[mine_r], send.at[9], recv_term, "resp", p),
     )
-    dk_half[...] = (dk_acc[...] * scale).astype(HALF)
-    dv_half[...] = dv_acc[...].astype(HALF)
-
-    def give_own(p):
-        part_rows = pl.ds(pl.multiple_of(p * rows, rows), rows)
-        start(dk_half.at[part_rows, :], dkv_out.at[0, :, own_head], send.at[10], recv_dkv.at[0], "heads", p)
-        start(dv_half.at[part_rows, :], dkv_out.at[1, :, own_head], send.at[11], recv_dkv.at[1], "heads", p)
-
-    others(heads, me, give_own)
     put = [
         pltpu.make_async_copy(dq_all.at[own_rows, :], dq_out.at[:, own_cols], local.at[0]),
         pltpu.make_async_copy(dk_half.at[own_rows, :], dkv_out.at[0, :, own_head], local.at[1]),

time: 66.4 us -> 66.6 us (level)
  no operation moved by 1% of the time
where the time goes in v4:
time: 66.6 us; the launch traced here: 66.4 us
  Pallas kernels  62.2 us (93%)
  local copies, waits for them, and re-layouts  2.29 us (3%)
  between operations  1.94 us (3%)
    pallas_call x1, Pallas kernels, on_device(): pl.pallas_call(functools.partial(kernel, sizes), out_shape=(jax.ShapeDtyp...  62.2 us

profile of v4, /device:TPU:1, one launch (start us, length us, event | category | flops | bytes accessed | tf_op | source)
XLA Modules:
  0.0 66.4 jit_solution(1833958010380505891)
XLA Ops:
  1.9 62.2 %shard_map.128 = (bf16[64,8192]{1,0:T(8,128)(2,1)S(1)}, bf16[2,64,1024]{2,1,0:T(8,128)(2,1)S(1)}, bf16[2,8,4,128]{3,2,1,0:T(4,128)(2,1)S(1)}) custom-call(s32[1]{0:T(128)S(6)} %copy.15.prompt_id, s32[1]{0:T(128)S(6)} %copy.16.length, bf16[64,8192]{1,0:T(8,128)(2,1)} %bitcast.11, bf16[64,8192]{1,0:T(8,128)(2,1)} %bitcast.12, bf16[64,8192]{1,0:T(8,128)(2,1)} %bitcast.13, ...), custom_call_target="tpu_custom_call" | custom-call | tf_op jit(solution)/shard_map/pallas_call | solution.py:458
  64.2 0.6 slice_bitcast_fusion
  64.8 0.7 %fusion = (bf16[1,64,1024]{2,1,0:T(8,128)(2,1)}, bf16[1,64,1024]{2,1,0:T(8,128)(2,1)}) fusion(bf16[2,64,1024]{2,1,0:T(8,128)(2,1)S(1)} %get-tuple-element.9), kind=kLoop, calls=%fused_computation.2 | loop fusion | bytes 524288 | tf_op jit(solution)/shard_map/slice | solution.py:528
  65.5 1.0 %copy.17 = bf16[1,64,8192]{2,1,0:T(8,128)(2,1)} copy(bf16[1,64,8192]{2,1,0:T(8,128)(2,1)S(1)} %bitcast.10) | data formatting | bytes 2097152
